TPU v7x, 256 devices: a whole 4x4x8 slice. The times are simulated.
256 devices in a mesh: dp: 2 (over y_lo), stretch: 16 (over x, y_hi, core), head: 8 (over z).
Axes of the slice: x: 4, y: 4 (y_hi: 2, y_lo: 2; y = y_hi * 2 + y_lo), z: 8, core: 2. Of those that a mesh axis runs over, the one named last changes fastest.
Arguments:
- queries: bfloat16 [32768, 2048], P(('dp', 'stretch', 'head')), parts along dimension 0, may hold values from -6 to 6
- key_heads: bfloat16 [32768, 256], P(('dp', 'stretch', 'head')), parts along dimension 0, may hold values from -6 to 6
- value_heads: bfloat16 [32768, 256], P(('dp', 'stretch', 'head')), parts along dimension 0, may hold values from -6 to 6
- out_grad: bfloat16 [32768, 2048], P(('dp', 'stretch', 'head')), parts along dimension 0, may hold values from -6 to 6
- lengths: int32 [128], P('dp'), parts along dimension 0, may hold values from 1 to 2048, 16384 in all
Outputs:
- attended: bfloat16 [32768, 2048], P(('dp', 'stretch', 'head')), parts along dimension 0
- query_grad: bfloat16 [32768, 2048], P(('dp', 'stretch', 'head')), parts along dimension 0
- key_grad: bfloat16 [32768, 256], P(('dp', 'stretch', 'head')), parts along dimension 0
- value_grad: bfloat16 [32768, 256], P(('dp', 'stretch', 'head')), parts along dimension 0
There are 2 independent parts, one for each index of `dp`. A program takes and returns all parts, laid end to end along the dimension named above; each array names one. Nothing has to cross between parts.
Inputs may be any that keep to these rules, and one draw needn't show every extreme that they name: The lengths sum to 16384.
All inputs are finite; a program needn't handle non-finite values.
Results may differ from a plain program's by a relative error of at most 0.029.
Values may be sent and summed in bfloat16 or wider, within the bound.
No kernel may reach another device: no remote copies, remote signals or barrier semaphores. Data moves between devices by JAX's collectives and lax.ppermute only.
A program may use at most 128 MiB of HBM per device.

v0:
```python
import jax
import jax.numpy as jnp
from jax import lax
from jax.experimental import pallas as pl
from jax.experimental.pallas import tpu as pltpu
from jax.sharding import PartitionSpec as P

HD = 128
GROUP = 8
ROWS = 128
WIDE = GROUP * HD
LANES = GROUP * ROWS
RING = 8
DISTANCES = ((0, 1), (-1, -2), (2, 3), (-3, -4))
REACH = 17 * ROWS
TILE = 8 * ROWS
SPAN = 2048
SCALE = HD**-0.5
EXP2 = SCALE * 1.4426950408889634
LOW = -1e30


def dot(x, y, cx, cy):
    return lax.dot_general(
        x, y, (((cx,), (cy,)), ((), ())), preferred_element_type=jnp.float32
    )


def attend_kernel(info, lengths, qo, go, come, *refs):
    kv_refs = refs[:8]
    att_own, dq_own, other = refs[8:11]
    part_refs = refs[11:21]
    q_s, g_s, k_s, v_s, dk_s, dv_s, s_s, w_s, o_s, top_s, sum_s, high_s, low_s, res_s = refs[21:]
    h, core = info[0], lax.rem(info[1], 2)
    origin = (info[1] // 2 - 1) * SPAN
    base = pl.multiple_of(core * WIDE, WIDE)
    for n in range(GROUP):
        rows = slice(n * ROWS, (n + 1) * ROWS)
        q_s[0, rows, :] = qo[:, pl.ds(base + n * HD, HD)]
        g_s[0, rows, :] = go[:, pl.ds(base + n * HD, HD)]
        q_s[1, rows, :] = come[:, n * HD : (n + 1) * HD]
        g_s[1, rows, :] = come[:, WIDE + n * HD : WIDE + (n + 1) * HD]
    sign = 1 - 2 * lax.rem(h + core, 2)

    def row_of(distance, past, piece):
        j = lax.rem(h + sign * distance + RING, RING)
        side = core if piece == 0 else 1 - core
        chunk = j + 8 * side + (0 if past else 16)
        return pl.multiple_of(chunk * ROWS, ROWS)

    places = [
        (4 * past + i, 2 * at + piece, row_of(distance, past, piece))
        for past in range(2)
        for i, pair in enumerate(DISTANCES)
        for at, distance in enumerate(pair)
        for piece in range(2)
    ]
    for array, at, row in places:
        k_s[pl.ds(row, ROWS), :] = kv_refs[array][at * ROWS : (at + 1) * ROWS, :HD]
        v_s[pl.ds(row, ROWS), :] = kv_refs[array][at * ROWS : (at + 1) * ROWS, HD:]
    dk_s[...] = jnp.zeros_like(dk_s)
    dv_s[...] = jnp.zeros_like(dv_s)

    @pl.loop(0, 2)
    def _(slot):
        side = core + slot * (1 - 2 * core)
        first = SPAN + (h + 8 * side) * ROWS
        place = first + lax.broadcasted_iota(jnp.int32, (1, ROWS), 1)

        begin = reach = -origin
        start = jnp.full((1, ROWS), begin, jnp.int32)
        for i in range(lengths.shape[0] - 1):
            begin += lengths[i]
            reach = jnp.where(begin <= first, begin, reach)
            start = jnp.where(begin <= place, begin, start)
        low = reach // ROWS * ROWS
        chunks = (first + ROWS - low) // ROWS
        tiles = chunks // 8

        def over_keys(visit):
            def tile(b, carry):
                visit(pl.multiple_of(b * TILE, TILE), TILE)
                return carry

            lax.fori_loop(0, tiles, tile, 0)

            @pl.when(chunks % 8 >= 4)
            def _():
                visit(pl.multiple_of(tiles * TILE, TILE), 4 * ROWS)

            @pl.when(chunks % 4 >= 2)
            def _():
                visit(pl.multiple_of(chunks // 4 * 4 * ROWS, 4 * ROWS), 2 * ROWS)

            @pl.when(chunks % 2 == 1)
            def _():
                visit(pl.multiple_of((chunks - 1) * ROWS, ROWS), ROWS)

        start = jnp.concatenate([start] * GROUP, axis=1)
        place = jnp.concatenate([place] * GROUP, axis=1)

        def scores(at, size):
            row = pl.multiple_of(low + at, ROWS)
            raw = dot(k_s[pl.ds(row, size), :], q_s[slot], 1, 1)
            key_place = row + lax.broadcasted_iota(jnp.int32, (size, LANES), 0)
            raw = jnp.where((key_place >= start) & (key_place <= place), raw, LOW)
            s_s[pl.ds(at, size), :] = raw
            top_s[...] = jnp.maximum(top_s[...], jnp.max(raw.reshape(size // 8, 8, LANES), axis=0))

        top_s[...] = jnp.full_like(top_s, LOW)
        over_keys(scores)
        top = jnp.max(top_s[...], axis=0, keepdims=True)
        sum_s[...] = jnp.zeros_like(sum_s)
        o_s[...] = jnp.zeros_like(o_s)

        def forward(at, size):
            row = pl.multiple_of(low + at, ROWS)
            weight = jnp.exp2((s_s[pl.ds(at, size), :] - top) * EXP2)
            rounded = weight.astype(jnp.bfloat16)
            w_s[pl.ds(at, size), :] = rounded
            o_s[...] += dot(v_s[pl.ds(row, size), :], rounded, 0, 0)
            sum_s[...] += jnp.sum(weight.reshape(size // 8, 8, LANES), axis=0)

        over_keys(forward)
        inverse = 1.0 / jnp.sum(sum_s[...], axis=0, keepdims=True)
        wide = jnp.broadcast_to(inverse, (8, LANES))
        for n in range(GROUP):
            cols = slice(n * HD, (n + 1) * HD)
            rows = slice(n * ROWS, (n + 1) * ROWS)
            att = jnp.transpose((o_s[:, rows] * inverse[:, rows]).astype(jnp.bfloat16))
            res_s[slot, :, cols] = att
            column = jnp.transpose(wide[:, rows])[:, :1]
            scaled = (g_s[slot, rows, :].astype(jnp.float32) * column).astype(jnp.bfloat16)
            g_s[slot, rows, :] = scaled
            product = att.astype(jnp.float32) * scaled.astype(jnp.float32)
            high_s[rows, :] = product.astype(jnp.bfloat16)
            low_s[rows, :] = (product - product.astype(jnp.bfloat16).astype(jnp.float32)).astype(jnp.bfloat16)
        ones = jnp.ones((8, HD), jnp.bfloat16)
        correction = (dot(ones, high_s[...], 1, 1) + dot(ones, low_s[...], 1, 1))[:1]
        o_s[...] = jnp.zeros_like(o_s)

        def backward(at, size):
            keys = pl.ds(pl.multiple_of(low + at, ROWS), size)
            weight = w_s[pl.ds(at, size), :]
            weight_grad = dot(v_s[keys, :], g_s[slot], 1, 1)
            score_grad = weight.astype(jnp.float32) * (weight_grad - correction)
            score_grad = score_grad.astype(jnp.bfloat16)
            dv_s[keys, :] += dot(weight, g_s[slot], 1, 0)
            dk_s[keys, :] += dot(score_grad, q_s[slot], 1, 0)
            o_s[...] += dot(k_s[keys, :], score_grad, 0, 0)

        over_keys(backward)
        for n in range(GROUP):
            rows = slice(n * ROWS, (n + 1) * ROWS)
            query_grad = jnp.transpose((o_s[:, rows] * SCALE).astype(jnp.bfloat16))
            res_s[slot, :, WIDE + n * HD : WIDE + (n + 1) * HD] = query_grad

    att_own[...] = res_s[0, :, :WIDE]
    dq_own[...] = res_s[0, :, WIDE:]
    other[...] = res_s[1]

    for array, at, row in places:
        line, i = divmod(array, 4)
        part = part_refs[5 * line + i + (0 if i == 0 and at < 2 else 1)]
        at = at % 2 if i == 0 else at
        rows = slice(at * ROWS, (at + 1) * ROWS)
        part[rows, :HD] = (dk_s[pl.ds(row, ROWS), :] * SCALE).astype(part.dtype)
        part[rows, HD:] = dv_s[pl.ds(row, ROWS), :].astype(part.dtype)


def attend(info, lengths, operands):
    bf16 = jnp.bfloat16
    side = jax.ShapeDtypeStruct((ROWS, WIDE), bf16)
    near = [
        jax.ShapeDtypeStruct((2 * ROWS, 2 * HD), jnp.float32),
        jax.ShapeDtypeStruct((2 * ROWS, 2 * HD), bf16),
    ]
    parts = near + [jax.ShapeDtypeStruct((4 * ROWS, 2 * HD), bf16)] * 3
    whole = pl.BlockSpec(memory_space=pltpu.VMEM)
    keys = 2 * SPAN
    return pl.pallas_call(
        attend_kernel,
        in_specs=[pl.BlockSpec(memory_space=pltpu.SMEM)] * 2 + [whole] * len(operands),
        out_specs=[whole] * 13,
        out_shape=[side, side, jax.ShapeDtypeStruct((ROWS, 2 * WIDE), bf16)] + parts * 2,
        scratch_shapes=[
            pltpu.VMEM((2, LANES, HD), bf16),
            pltpu.VMEM((2, LANES, HD), bf16),
            pltpu.VMEM((keys, HD), bf16),
            pltpu.VMEM((keys, HD), bf16),
            pltpu.VMEM((keys, HD), jnp.float32),
            pltpu.VMEM((keys, HD), jnp.float32),
            pltpu.VMEM((REACH, LANES), jnp.float32),
            pltpu.VMEM((REACH, LANES), bf16),
            pltpu.VMEM((HD, LANES), jnp.float32),
            pltpu.VMEM((8, LANES), jnp.float32),
            pltpu.VMEM((8, LANES), jnp.float32),
            pltpu.VMEM((LANES, HD), bf16),
            pltpu.VMEM((LANES, HD), bf16),
            pltpu.VMEM((2, ROWS, 2 * WIDE), bf16),
        ],
        compiler_params=pltpu.CompilerParams(vmem_limit_bytes=48 * 1024 * 1024),
        name="attend",
    )(info, lengths, *operands)


def join_kernel(info, att, dq, come, here, sent, other, att_out, dq_out, key_out, value_out):
    core = lax.rem(info[1], 2)
    own = pl.multiple_of(core * WIDE, WIDE)
    far = pl.multiple_of((1 - core) * WIDE, WIDE)
    att_out[:, pl.ds(own, WIDE)] = att[...]
    att_out[:, pl.ds(far, WIDE)] = come[:, :WIDE]
    dq_out[:, pl.ds(own, WIDE)] = dq[...]
    dq_out[:, pl.ds(far, WIDE)] = come[:, WIDE:]
    mine = (here[...] + sent[...].astype(jnp.float32)).astype(jnp.bfloat16)
    own = pl.multiple_of(core * HD, HD)
    far = pl.multiple_of((1 - core) * HD, HD)
    key_out[:, pl.ds(own, HD)] = mine[:, :HD]
    key_out[:, pl.ds(far, HD)] = other[:, :HD]
    value_out[:, pl.ds(own, HD)] = mine[:, HD:]
    value_out[:, pl.ds(far, HD)] = other[:, HD:]


def join(info, operands):
    whole = pl.BlockSpec(memory_space=pltpu.VMEM)
    long = jax.ShapeDtypeStruct((ROWS, 2 * WIDE), jnp.bfloat16)
    short = jax.ShapeDtypeStruct((ROWS, 2 * HD), jnp.bfloat16)
    return pl.pallas_call(
        join_kernel,
        in_specs=[pl.BlockSpec(memory_space=pltpu.SMEM)] + [whole] * len(operands),
        out_specs=[whole] * 4,
        out_shape=[long, long, short, short],
        compiler_params=pltpu.CompilerParams(vmem_limit_bytes=16 * 1024 * 1024),
        name="join",
    )(info, *operands)


def add(*terms):
    return sum(term.astype(jnp.float32) for term in terms).astype(jnp.bfloat16)


def body(queries, key_heads, value_heads, out_grad, lengths):
    count = lax.axis_size("stretch")
    stretch = lax.axis_index("stretch")
    h = lax.axis_index("head")
    core = lax.rem(stretch, 2)
    swap = [(s, s ^ 1) for s in range(count)]
    later = [(s, s + 2) for s in range(count - 2)]
    earlier = [(s + 2, s) for s in range(count - 2)]
    above, below = [
        [
            (s * RING + i, s * RING + (i + (1 if (s + i + turn) % 2 == 0 else -1)) % RING)
            for s in range(count)
            for i in range(RING)
        ]
        for turn in range(2)
    ]

    middle = 2 * ROWS

    def exchange(array, pairs):
        return lax.ppermute(array, ("stretch", "head"), pairs)

    def gather(held, neighbour):
        near = jnp.concatenate([held, neighbour], axis=0)
        second = exchange(near, below)
        third = exchange(second, above)
        return [near, second, third, exchange(third, below)]

    def scatter(here, near, second, third, fourth):
        third = add(third, exchange(fourth, below))
        second = add(second, exchange(third, above))
        come = exchange(second, below)
        return here + come[:middle].astype(jnp.float32), add(near, come[middle:])

    def half(array, which, width):
        return lax.dynamic_slice_in_dim(array, which * width, width, axis=1)

    def pair(which):
        return jnp.concatenate([half(key_heads, which, HD), half(value_heads, which, HD)], axis=1)

    own = jnp.concatenate([pair(core), lax.ppermute(pair(1 - core), "stretch", swap)], axis=0)
    leaving = [half(array, 1 - core, WIDE) for array in (queries, out_grad)]
    come = lax.ppermute(jnp.concatenate(leaving, axis=1), "stretch", swap)
    past = lax.ppermute(own, "stretch", later)
    slant = [(a, b + 2 * RING) for a, b in above if b + 2 * RING < count * RING]
    slanted = exchange(own, slant)
    info = jnp.stack([h, stretch]).astype(jnp.int32)
    operands = [queries, out_grad, come, *gather(own, exchange(own, above)), *gather(past, slanted)]
    outs = attend(info, lengths, operands)
    past_here, past_near = scatter(*outs[8:13])
    here, near = scatter(*outs[3:8])
    past_sum = past_here + exchange(past_near, above).astype(jnp.float32)
    sent_back = lax.ppermute(past_sum.astype(jnp.bfloat16), "stretch", earlier)
    near, swapped = lax.optimization_barrier((near, outs[2]))
    here = here + exchange(near, above).astype(jnp.float32)
    swapped = lax.ppermute(swapped, "stretch", swap)
    other = lax.ppermute(add(here[ROWS:], sent_back[ROWS:]), "stretch", swap)
    return join(info, [outs[0], outs[1], swapped, here[:ROWS], sent_back[:ROWS], other])


def solution(mesh):
    spec = P(("dp", "stretch", "head"), None)
    return jax.shard_map(
        body,
        mesh=mesh,
        in_specs=(spec, spec, spec, spec, P("dp")),
        out_specs=(spec,) * 4,
        check_vma=False,
    )
```

profile of v0, /device:TPU:7, one launch (start us, length us, event | category | flops | bytes accessed | tf_op | source)
XLA Modules:
  0.0 107.7 jit_solution(17379204665204838761)
XLA Ops:
  0.6 0.8 constant_dynamic-slice_fusion.2
  1.5 0.8 collective-permute-start.1
  2.3 0.9 collective-permute-done.1
  3.2 5.7 %collective-permute-start.2 = (bf16[256,256]{1,0:T(8,128)(2,1)S(1)}, bf16[256,256]{1,0:T(8,128)(2,1)S(1)}, u32[]{:S(2)}, u32[]{:S(2)}) collective-permute-start(bf16[256,256]{1,0:T(8,128)(2,1)S(1)} %pad_maximum_fusion.2), channel_id=1, source_target_pairs={{0,1},{1,0},{2,3},{3,2},{4,5},{5,4},{6,7},{7,6},{8,15},{9,10},{10,... | collective-permute-start | bytes 393224 | tf_op jit(solution)/shard_map/ppermute | solution.py:262
  8.8 4.8 %collective-permute-start.6 = (bf16[256,256]{1,0:T(8,128)(2,1)S(1)}, bf16[256,256]{1,0:T(8,128)(2,1)S(1)}, u32[]{:S(2)}, u32[]{:S(2)}) collective-permute-start(bf16[256,256]{1,0:T(8,128)(2,1)S(1)} %pad_maximum_fusion.2), channel_id=1, source_target_pairs={{0,16},{8,24},{16,32},{24,40},{32,48},{40,56},{48,64},{56,72},{64,... | collective-permute-start | bytes 393224 | tf_op jit(solution)/shard_map/ppermute | solution.py:285
  13.7 0.0 copy-start.2
  13.7 0.0 copy-start
  13.7 2.1 %collective-permute-start.7 = (bf16[256,256]{1,0:T(8,128)(2,1)S(1)}, bf16[256,256]{1,0:T(8,128)(2,1)S(1)}, u32[]{:S(2)}, u32[]{:S(2)}) collective-permute-start(bf16[256,256]{1,0:T(8,128)(2,1)S(1)} %pad_maximum_fusion.2), channel_id=1, source_target_pairs={{0,17},{1,16},{2,19},{3,18},{4,21},{5,20},{6,23},{7,22},{8,31},{9,... | collective-permute-start | bytes 393224 | tf_op jit(solution)/shard_map/ppermute | solution.py:262
  15.7 0.0 collective-permute-done.2
  15.8 0.1 collective-permute-start.3
  15.9 1.1 collective-permute-done.6
  17.0 8.2 %collective-permute-done.7 = bf16[256,256]{1,0:T(8,128)(2,1)S(1)} collective-permute-done((bf16[256,256]{1,0:T(8,128)(2,1)S(1)}, bf16[256,256]{1,0:T(8,128)(2,1)S(1)}, u32[]{:S(2)}, u32[]{:S(2)}) %collective-permute-start.7) | collective-permute-done | bytes 131104 | tf_op jit(solution)/shard_map/ppermute | solution.py:262
  25.1 0.1 collective-permute-start.8
  25.2 0.0 copy-done.2
  25.2 0.0 copy-done
  25.3 1.5 %collective-permute-start = (bf16[128,2048]{1,0:T(8,128)(2,1)S(1)}, bf16[128,2048]{1,0:T(8,128)(2,1)}, u32[]{:S(2)}, u32[]{:S(2)}) collective-permute-start(bf16[128,2048]{1,0:T(8,128)(2,1)S(1)} %pad_maximum_fusion), channel_id=1, source_target_pairs={{0,8},{8,0},{16,24},{24,16},{32,40},{40,32},{48,56},{56,48},{64,72... | collective-permute-start | bytes 1572872 | tf_op jit(solution)/shard_map/ppermute | solution.py:284
  26.9 0.0 collective-permute-done.3.refs_1_
  26.9 0.0 collective-permute-start.4
  26.9 4.3 %collective-permute-done.8.refs_5_ = bf16[512,256]{1,0:T(8,128)(2,1)S(1)} collective-permute-done((bf16[512,256]{1,0:T(8,128)(2,1)S(1)}, bf16[512,256]{1,0:T(8,128)(2,1)S(1)}, u32[]{:S(2)}, u32[]{:S(2)}) %collective-permute-start.8) | collective-permute-done | bytes 262176 | tf_op jit(solution)/shard_map/ppermute | solution.py:262
  31.2 0.0 collective-permute-start.9
  31.2 2.1 %collective-permute-done.4.refs_2_ = bf16[512,256]{1,0:T(8,128)(2,1)S(1)} collective-permute-done((bf16[512,256]{1,0:T(8,128)(2,1)S(1)}, bf16[512,256]{1,0:T(8,128)(2,1)S(1)}, u32[]{:S(2)}, u32[]{:S(2)}) %collective-permute-start.4) | collective-permute-done | bytes 262176 | tf_op jit(solution)/shard_map/ppermute | solution.py:262
  33.3 0.0 collective-permute-start.5
  33.3 4.3 %collective-permute-done.9.refs_6_ = bf16[512,256]{1,0:T(8,128)(2,1)S(1)} collective-permute-done((bf16[512,256]{1,0:T(8,128)(2,1)S(1)}, bf16[512,256]{1,0:T(8,128)(2,1)S(1)}, u32[]{:S(2)}, u32[]{:S(2)}) %collective-permute-start.9) | collective-permute-done | bytes 262176 | tf_op jit(solution)/shard_map/ppermute | solution.py:262
  37.7 0.0 collective-permute-start.10
  37.7 0.0 copy-start.1
  37.7 0.1 pad_add_fusion.info
  37.7 0.0 collective-permute-done.come
  37.7 3.4 %collective-permute-done.5.refs_3_ = bf16[512,256]{1,0:T(8,128)(2,1)S(1)} collective-permute-done((bf16[512,256]{1,0:T(8,128)(2,1)S(1)}, bf16[512,256]{1,0:T(8,128)(2,1)S(1)}, u32[]{:S(2)}, u32[]{:S(2)}) %collective-permute-start.5) | collective-permute-done | bytes 262176 | tf_op jit(solution)/shard_map/ppermute | solution.py:262
  41.2 3.0 %collective-permute-done.10.refs_7_ = bf16[512,256]{1,0:T(8,128)(2,1)S(1)} collective-permute-done((bf16[512,256]{1,0:T(8,128)(2,1)S(1)}, bf16[512,256]{1,0:T(8,128)(2,1)S(1)}, u32[]{:S(2)}, u32[]{:S(2)}) %collective-permute-start.10) | collective-permute-done | bytes 262176 | tf_op jit(solution)/shard_map/ppermute | solution.py:262
  44.2 0.0 copy-done.1
  44.2 10.7 %attend.1 = (bf16[128,1024]{1,0:T(8,128)(2,1)S(1)}, bf16[128,1024]{1,0:T(8,128)(2,1)S(1)}, bf16[128,2048]{1,0:T(8,128)(2,1)S(1)}, f32[256,256]{1,0:T(8,128)S(1)}...) custom-call(s32[2]{0:T(128)S(1)} %pad_add_fusion.info, ...), custom_call_target="tpu_custom_call" | custom-call | tf_op jit(solution)/shard_map/attend/pallas_call | solution.py:181
  54.8 0.5 collective-permute-start.16
  55.3 1.1 %collective-permute-start.11 = (bf16[512,256]{1,0:T(8,128)(2,1)S(1)}, bf16[512,256]{1,0:T(8,128)(2,1)S(1)}, u32[]{:S(2)}, u32[]{:S(2)}) collective-permute-start(bf16[512,256]{1,0:T(8,128)(2,1)S(1)} %get-tuple-element.24), channel_id=1, source_target_pairs={{0,7},{1,2},{2,1},{3,4},{4,3},{5,6},{6,5},{7,0},{8,9},{9,8},{10,11... | collective-permute-start | bytes 786440 | tf_op jit(solution)/shard_map/ppermute | solution.py:262
  56.4 3.8 %collective-permute-done.16 = bf16[512,256]{1,0:T(8,128)(2,1)S(1)} collective-permute-done((bf16[512,256]{1,0:T(8,128)(2,1)S(1)}, bf16[512,256]{1,0:T(8,128)(2,1)S(1)}, u32[]{:S(2)}, u32[]{:S(2)}) %collective-permute-start.16) | collective-permute-done | bytes 262176 | tf_op jit(solution)/shard_map/ppermute | solution.py:262
  60.2 0.1 add_convert_fusion.1
  60.2 7.0 %collective-permute-start.17 = (bf16[512,256]{1,0:T(8,128)(2,1)S(1)}, bf16[512,256]{1,0:T(8,128)(2,1)S(1)}, u32[]{:S(2)}, u32[]{:S(2)}) collective-permute-start(bf16[512,256]{1,0:T(8,128)(2,1)S(1)} %add_convert_fusion.1), channel_id=1, source_target_pairs={{0,1},{1,0},{2,3},{3,2},{4,5},{5,4},{6,7},{7,6},{8,15},{9,10},{10,... | collective-permute-start | bytes 786440 | tf_op jit(solution)/shard_map/ppermute | solution.py:262
  67.2 0.0 collective-permute-done.11
  67.2 0.1 add_convert_fusion.3
  67.3 2.7 %collective-permute-start.12 = (bf16[512,256]{1,0:T(8,128)(2,1)S(1)}, bf16[512,256]{1,0:T(8,128)(2,1)S(1)}, u32[]{:S(2)}, u32[]{:S(2)}) collective-permute-start(bf16[512,256]{1,0:T(8,128)(2,1)S(1)} %add_convert_fusion.3), channel_id=1, source_target_pairs={{0,1},{1,0},{2,3},{3,2},{4,5},{5,4},{6,7},{7,6},{8,15},{9,10},{10,... | collective-permute-start | bytes 786440 | tf_op jit(solution)/shard_map/ppermute | solution.py:262
  70.0 3.0 %collective-permute-done.17 = bf16[512,256]{1,0:T(8,128)(2,1)S(1)} collective-permute-done((bf16[512,256]{1,0:T(8,128)(2,1)S(1)}, bf16[512,256]{1,0:T(8,128)(2,1)S(1)}, u32[]{:S(2)}, u32[]{:S(2)}) %collective-permute-start.17) | collective-permute-done | bytes 262176 | tf_op jit(solution)/shard_map/ppermute | solution.py:262
  73.0 0.1 add_convert_fusion
  73.0 0.3 collective-permute-start.18
  73.3 5.2 %collective-permute-done.12 = bf16[512,256]{1,0:T(8,128)(2,1)S(1)} collective-permute-done((bf16[512,256]{1,0:T(8,128)(2,1)S(1)}, bf16[512,256]{1,0:T(8,128)(2,1)S(1)}, u32[]{:S(2)}, u32[]{:S(2)}) %collective-permute-start.12) | collective-permute-done | bytes 262176 | tf_op jit(solution)/shard_map/ppermute | solution.py:262
  78.6 0.1 add_convert_fusion.2
  78.6 0.1 collective-permute-start.13
  78.7 0.1 collective-permute-done.18
  78.9 2.4 %collective-permute-start.19 = (bf16[256,256]{1,0:T(8,128)(2,1)S(1)}, bf16[256,256]{1,0:T(8,128)(2,1)S(1)}, u32[]{:S(2)}, u32[]{:S(2)}) collective-permute-start(bf16[256,256]{1,0:T(8,128)(2,1)S(1)} %add_convert_fusion.5), channel_id=1, source_target_pairs={{0,1},{1,0},{2,3},{3,2},{4,5},{5,4},{6,7},{7,6},{8,15},{9,10},{10,... | collective-permute-start | bytes 393224 | tf_op jit(solution)/shard_map/ppermute | solution.py:262
  81.3 4.2 %collective-permute-done.13 = bf16[512,256]{1,0:T(8,128)(2,1)S(1)} collective-permute-done((bf16[512,256]{1,0:T(8,128)(2,1)S(1)}, bf16[512,256]{1,0:T(8,128)(2,1)S(1)}, u32[]{:S(2)}, u32[]{:S(2)}) %collective-permute-start.13) | collective-permute-done | bytes 262176 | tf_op jit(solution)/shard_map/ppermute | solution.py:262
  85.6 3.4 %collective-permute-start.15 = (bf16[256,256]{1,0:T(8,128)(2,1)S(1)}, bf16[256,256]{1,0:T(8,128)(2,1)S(1)}, u32[]{:S(2)}, u32[]{:S(2)}) collective-permute-start(bf16[256,256]{1,0:T(8,128)(2,1)S(1)} %add_convert_fusion.6), channel_id=1, source_target_pairs={{0,1},{1,0},{2,3},{3,2},{4,5},{5,4},{6,7},{7,6},{8,15},{9,10},{10,... | collective-permute-start | bytes 393224 | tf_op jit(solution)/shard_map/ppermute | solution.py:262
  89.0 6.7 %collective-permute-start.14 = (bf16[128,2048]{1,0:T(8,128)(2,1)S(1)}, bf16[128,2048]{1,0:T(8,128)(2,1)S(1)}, u32[]{:S(2)}, u32[]{:S(2)}) collective-permute-start(bf16[128,2048]{1,0:T(8,128)(2,1)S(1)} %get-tuple-element.26), channel_id=1, source_target_pairs={{0,8},{8,0},{16,24},{24,16},{32,40},{40,32},{48,56},{56,48},{64,72... | collective-permute-start | bytes 1572872 | tf_op jit(solution)/shard_map/ppermute | solution.py:297
  95.7 0.0 collective-permute-done.19
  95.8 1.9 %collective-permute-start.20 = (bf16[256,256]{1,0:T(8,128)(2,1)S(1)}, bf16[256,256]{1,0:T(8,128)(2,1)S(1)}, u32[]{:S(2)}, u32[]{:S(2)}) collective-permute-start(bf16[256,256]{1,0:T(8,128)(2,1)S(1)} %add_convert_fusion.4), channel_id=1, source_target_pairs={{16,0},{24,8},{32,16},{40,24},{48,32},{56,40},{64,48},{72,56},{80,... | collective-permute-start | bytes 393224 | tf_op jit(solution)/shard_map/ppermute | solution.py:294
  97.7 0.0 collective-permute-done.15
  97.7 6.0 %collective-permute-done.20 = bf16[256,256]{1,0:T(8,128)(2,1)S(1)} collective-permute-done((bf16[256,256]{1,0:T(8,128)(2,1)S(1)}, bf16[256,256]{1,0:T(8,128)(2,1)S(1)}, u32[]{:S(2)}, u32[]{:S(2)}) %collective-permute-start.20) | collective-permute-done | bytes 131104 | tf_op jit(solution)/shard_map/ppermute | solution.py:294
  103.7 1.5 %collective-permute-start.21 = (bf16[128,256]{1,0:T(8,128)(2,1)S(1)}, bf16[128,256]{1,0:T(8,128)(2,1)S(1)}, u32[]{:S(2)}, u32[]{:S(2)}) collective-permute-start(bf16[128,256]{1,0:T(8,128)(2,1)S(1)} %get-tuple-element.34), channel_id=1, source_target_pairs={{0,8},{8,0},{16,24},{24,16},{32,40},{40,32},{48,56},{56,48},{64,72... | collective-permute-start | bytes 196616 | tf_op jit(solution)/shard_map/ppermute | solution.py:298
  105.2 0.9 collective-permute-done.21.other
  106.1 0.0 collective-permute-done.14.come
  106.1 1.6 %join.1 = (bf16[128,2048]{1,0:T(8,128)(2,1)}, bf16[128,2048]{1,0:T(8,128)(2,1)}, bf16[128,256]{1,0:T(8,128)(2,1)}, bf16[128,256]{1,0:T(8,128)(2,1)}) custom-call(s32[2]{0:T(128)S(1)} %pad_add_fusion.info, bf16[128,1024]{1,0:T(8,128)(2,1)S(1)} %get-tuple-element.19.att, bf16[128,1024]{1,0:T(8,128)(2,1)S(1)} %get-tuple-element.20.dq, ...), custom_call_target="tpu_custom_call" | custom-call | tf_op jit(solution)/shard_map/join/pallas_call | solution.py:228
  (13 shorter events, 0.3 us)
Async XLA Ops:
  1.5 1.7 %collective-permute-start.1 = (bf16[128,256]{1,0:T(8,128)(2,1)S(1)}, bf16[128,256]{1,0:T(8,128)(2,1)S(1)}, u32[]{:S(2)}, u32[]{:S(2)}) collective-permute-start(bf16[128,256]{1,0:T(8,128)(2,1)S(1)} %pad_maximum_fusion.3), channel_id=1, source_target_pairs={{0,8},{8,0},{16,24},{24,16},{32,40},{40,32},{48,56},{56,48},{64,72... | collective-permute-start | bytes 196616 | tf_op jit(solution)/shard_map/ppermute | solution.py:282
  3.2 12.6 %collective-permute-start.2 = (bf16[256,256]{1,0:T(8,128)(2,1)S(1)}, bf16[256,256]{1,0:T(8,128)(2,1)S(1)}, u32[]{:S(2)}, u32[]{:S(2)}) collective-permute-start(bf16[256,256]{1,0:T(8,128)(2,1)S(1)} %pad_maximum_fusion.2), channel_id=1, source_target_pairs={{0,1},{1,0},{2,3},{3,2},{4,5},{5,4},{6,7},{7,6},{8,15},{9,10},{10,... | collective-permute-start | bytes 393224 | tf_op jit(solution)/shard_map/ppermute | solution.py:262
  8.8 8.1 %collective-permute-start.6 = (bf16[256,256]{1,0:T(8,128)(2,1)S(1)}, bf16[256,256]{1,0:T(8,128)(2,1)S(1)}, u32[]{:S(2)}, u32[]{:S(2)}) collective-permute-start(bf16[256,256]{1,0:T(8,128)(2,1)S(1)} %pad_maximum_fusion.2), channel_id=1, source_target_pairs={{0,16},{8,24},{16,32},{24,40},{32,48},{40,56},{48,64},{56,72},{64,... | collective-permute-start | bytes 393224 | tf_op jit(solution)/shard_map/ppermute | solution.py:285
  13.7 11.6 %copy-start.2 = (bf16[128,2048]{1,0:T(8,128)(2,1)S(1)}, bf16[128,2048]{1,0:T(8,128)(2,1)}, u32[]{:S(2)}) copy-start(bf16[128,2048]{1,0:T(8,128)(2,1)} %go.1) | copy-start | bytes 1572868
  13.7 11.6 %copy-start = (bf16[128,2048]{1,0:T(8,128)(2,1)S(1)}, bf16[128,2048]{1,0:T(8,128)(2,1)}, u32[]{:S(2)}) copy-start(bf16[128,2048]{1,0:T(8,128)(2,1)} %qo.1) | copy-start | bytes 1572868
  13.7 11.4 %collective-permute-start.7 = (bf16[256,256]{1,0:T(8,128)(2,1)S(1)}, bf16[256,256]{1,0:T(8,128)(2,1)S(1)}, u32[]{:S(2)}, u32[]{:S(2)}) collective-permute-start(bf16[256,256]{1,0:T(8,128)(2,1)S(1)} %pad_maximum_fusion.2), channel_id=1, source_target_pairs={{0,17},{1,16},{2,19},{3,18},{4,21},{5,20},{6,23},{7,22},{8,31},{9,... | collective-permute-start | bytes 393224 | tf_op jit(solution)/shard_map/ppermute | solution.py:262
  15.8 11.1 %collective-permute-start.3 = (bf16[512,256]{1,0:T(8,128)(2,1)S(1)}, bf16[512,256]{1,0:T(8,128)(2,1)S(1)}, u32[]{:S(2)}, u32[]{:S(2)}) collective-permute-start(bf16[512,256]{1,0:T(8,128)(2,1)S(1)} %pad_maximum_fusion.1.refs_0_), channel_id=1, source_target_pairs={{0,7},{1,2},{2,1},{3,4},{4,3},{5,6},{6,5},{7,0},{8,9},{9,8},{10,11... | collective-permute-start | bytes 786440 | tf_op jit(solution)/shard_map/ppermute | solution.py:262
  25.1 6.1 %collective-permute-start.8 = (bf16[512,256]{1,0:T(8,128)(2,1)S(1)}, bf16[512,256]{1,0:T(8,128)(2,1)S(1)}, u32[]{:S(2)}, u32[]{:S(2)}) collective-permute-start(bf16[512,256]{1,0:T(8,128)(2,1)S(1)} %constant_dynamic-update-slice_fusion.refs_4_), channel_id=1, source_target_pairs={{0,7},{1,2},{2,1},{3,4},{4,3},{5,6},{6,5},{7,0},{8,9},{9,8},{10,11... | collective-permute-start | bytes 786440 | tf_op jit(solution)/shard_map/ppermute | solution.py:262
  25.3 12.4 %collective-permute-start = (bf16[128,2048]{1,0:T(8,128)(2,1)S(1)}, bf16[128,2048]{1,0:T(8,128)(2,1)}, u32[]{:S(2)}, u32[]{:S(2)}) collective-permute-start(bf16[128,2048]{1,0:T(8,128)(2,1)S(1)} %pad_maximum_fusion), channel_id=1, source_target_pairs={{0,8},{8,0},{16,24},{24,16},{32,40},{40,32},{48,56},{56,48},{64,72... | collective-permute-start | bytes 1572872 | tf_op jit(solution)/shard_map/ppermute | solution.py:284
  26.9 6.4 %collective-permute-start.4 = (bf16[512,256]{1,0:T(8,128)(2,1)S(1)}, bf16[512,256]{1,0:T(8,128)(2,1)S(1)}, u32[]{:S(2)}, u32[]{:S(2)}) collective-permute-start(bf16[512,256]{1,0:T(8,128)(2,1)S(1)} %collective-permute-done.3.refs_1_), channel_id=1, source_target_pairs={{0,1},{1,0},{2,3},{3,2},{4,5},{5,4},{6,7},{7,6},{8,15},{9,10},{10,... | collective-permute-start | bytes 786440 | tf_op jit(solution)/shard_map/ppermute | solution.py:262
  31.2 6.4 %collective-permute-start.9 = (bf16[512,256]{1,0:T(8,128)(2,1)S(1)}, bf16[512,256]{1,0:T(8,128)(2,1)S(1)}, u32[]{:S(2)}, u32[]{:S(2)}) collective-permute-start(bf16[512,256]{1,0:T(8,128)(2,1)S(1)} %collective-permute-done.8.refs_5_), channel_id=1, source_target_pairs={{0,1},{1,0},{2,3},{3,2},{4,5},{5,4},{6,7},{7,6},{8,15},{9,10},{10,... | collective-permute-start | bytes 786440 | tf_op jit(solution)/shard_map/ppermute | solution.py:262
  33.3 7.9 %collective-permute-start.5 = (bf16[512,256]{1,0:T(8,128)(2,1)S(1)}, bf16[512,256]{1,0:T(8,128)(2,1)S(1)}, u32[]{:S(2)}, u32[]{:S(2)}) collective-permute-start(bf16[512,256]{1,0:T(8,128)(2,1)S(1)} %collective-permute-done.4.refs_2_), channel_id=1, source_target_pairs={{0,7},{1,2},{2,1},{3,4},{4,3},{5,6},{6,5},{7,0},{8,9},{9,8},{10,11... | collective-permute-start | bytes 786440 | tf_op jit(solution)/shard_map/ppermute | solution.py:262
  37.7 6.5 %collective-permute-start.10 = (bf16[512,256]{1,0:T(8,128)(2,1)S(1)}, bf16[512,256]{1,0:T(8,128)(2,1)S(1)}, u32[]{:S(2)}, u32[]{:S(2)}) collective-permute-start(bf16[512,256]{1,0:T(8,128)(2,1)S(1)} %collective-permute-done.9.refs_6_), channel_id=1, source_target_pairs={{0,7},{1,2},{2,1},{3,4},{4,3},{5,6},{6,5},{7,0},{8,9},{9,8},{10,11... | collective-permute-start | bytes 786440 | tf_op jit(solution)/shard_map/ppermute | solution.py:262
  37.7 6.5 %copy-start.1 = (s32[64]{0:T(128)S(1)}, s32[64]{0:T(128)}, u32[]{:S(2)}) copy-start(s32[64]{0:T(128)} %lengths.1) | copy-start | bytes 772
  54.8 5.3 %collective-permute-start.16 = (bf16[512,256]{1,0:T(8,128)(2,1)S(1)}, bf16[512,256]{1,0:T(8,128)(2,1)S(1)}, u32[]{:S(2)}, u32[]{:S(2)}) collective-permute-start(bf16[512,256]{1,0:T(8,128)(2,1)S(1)} %get-tuple-element.32), channel_id=1, source_target_pairs={{0,7},{1,2},{2,1},{3,4},{4,3},{5,6},{6,5},{7,0},{8,9},{9,8},{10,11... | collective-permute-start | bytes 786440 | tf_op jit(solution)/shard_map/ppermute | solution.py:262
  55.3 11.9 %collective-permute-start.11 = (bf16[512,256]{1,0:T(8,128)(2,1)S(1)}, bf16[512,256]{1,0:T(8,128)(2,1)S(1)}, u32[]{:S(2)}, u32[]{:S(2)}) collective-permute-start(bf16[512,256]{1,0:T(8,128)(2,1)S(1)} %get-tuple-element.24), channel_id=1, source_target_pairs={{0,7},{1,2},{2,1},{3,4},{4,3},{5,6},{6,5},{7,0},{8,9},{9,8},{10,11... | collective-permute-start | bytes 786440 | tf_op jit(solution)/shard_map/ppermute | solution.py:262
  60.2 12.7 %collective-permute-start.17 = (bf16[512,256]{1,0:T(8,128)(2,1)S(1)}, bf16[512,256]{1,0:T(8,128)(2,1)S(1)}, u32[]{:S(2)}, u32[]{:S(2)}) collective-permute-start(bf16[512,256]{1,0:T(8,128)(2,1)S(1)} %add_convert_fusion.1), channel_id=1, source_target_pairs={{0,1},{1,0},{2,3},{3,2},{4,5},{5,4},{6,7},{7,6},{8,15},{9,10},{10,... | collective-permute-start | bytes 786440 | tf_op jit(solution)/shard_map/ppermute | solution.py:262
  67.3 11.3 %collective-permute-start.12 = (bf16[512,256]{1,0:T(8,128)(2,1)S(1)}, bf16[512,256]{1,0:T(8,128)(2,1)S(1)}, u32[]{:S(2)}, u32[]{:S(2)}) collective-permute-start(bf16[512,256]{1,0:T(8,128)(2,1)S(1)} %add_convert_fusion.3), channel_id=1, source_target_pairs={{0,1},{1,0},{2,3},{3,2},{4,5},{5,4},{6,7},{7,6},{8,15},{9,10},{10,... | collective-permute-start | bytes 786440 | tf_op jit(solution)/shard_map/ppermute | solution.py:262
  73.0 5.8 %collective-permute-start.18 = (bf16[512,256]{1,0:T(8,128)(2,1)S(1)}, bf16[512,256]{1,0:T(8,128)(2,1)S(1)}, u32[]{:S(2)}, u32[]{:S(2)}) collective-permute-start(bf16[512,256]{1,0:T(8,128)(2,1)S(1)} %add_convert_fusion), channel_id=1, source_target_pairs={{0,7},{1,2},{2,1},{3,4},{4,3},{5,6},{6,5},{7,0},{8,9},{9,8},{10,11... | collective-permute-start | bytes 786440 | tf_op jit(solution)/shard_map/ppermute | solution.py:262
  78.6 6.9 %collective-permute-start.13 = (bf16[512,256]{1,0:T(8,128)(2,1)S(1)}, bf16[512,256]{1,0:T(8,128)(2,1)S(1)}, u32[]{:S(2)}, u32[]{:S(2)}) collective-permute-start(bf16[512,256]{1,0:T(8,128)(2,1)S(1)} %add_convert_fusion.2), channel_id=1, source_target_pairs={{0,7},{1,2},{2,1},{3,4},{4,3},{5,6},{6,5},{7,0},{8,9},{9,8},{10,11... | collective-permute-start | bytes 786440 | tf_op jit(solution)/shard_map/ppermute | solution.py:262
  78.9 16.8 %collective-permute-start.19 = (bf16[256,256]{1,0:T(8,128)(2,1)S(1)}, bf16[256,256]{1,0:T(8,128)(2,1)S(1)}, u32[]{:S(2)}, u32[]{:S(2)}) collective-permute-start(bf16[256,256]{1,0:T(8,128)(2,1)S(1)} %add_convert_fusion.5), channel_id=1, source_target_pairs={{0,1},{1,0},{2,3},{3,2},{4,5},{5,4},{6,7},{7,6},{8,15},{9,10},{10,... | collective-permute-start | bytes 393224 | tf_op jit(solution)/shard_map/ppermute | solution.py:262
  85.6 12.1 %collective-permute-start.15 = (bf16[256,256]{1,0:T(8,128)(2,1)S(1)}, bf16[256,256]{1,0:T(8,128)(2,1)S(1)}, u32[]{:S(2)}, u32[]{:S(2)}) collective-permute-start(bf16[256,256]{1,0:T(8,128)(2,1)S(1)} %add_convert_fusion.6), channel_id=1, source_target_pairs={{0,1},{1,0},{2,3},{3,2},{4,5},{5,4},{6,7},{7,6},{8,15},{9,10},{10,... | collective-permute-start | bytes 393224 | tf_op jit(solution)/shard_map/ppermute | solution.py:262
  89.0 17.1 %collective-permute-start.14 = (bf16[128,2048]{1,0:T(8,128)(2,1)S(1)}, bf16[128,2048]{1,0:T(8,128)(2,1)S(1)}, u32[]{:S(2)}, u32[]{:S(2)}) collective-permute-start(bf16[128,2048]{1,0:T(8,128)(2,1)S(1)} %get-tuple-element.26), channel_id=1, source_target_pairs={{0,8},{8,0},{16,24},{24,16},{32,40},{40,32},{48,56},{56,48},{64,72... | collective-permute-start | bytes 1572872 | tf_op jit(solution)/shard_map/ppermute | solution.py:297
  95.8 7.9 %collective-permute-start.20 = (bf16[256,256]{1,0:T(8,128)(2,1)S(1)}, bf16[256,256]{1,0:T(8,128)(2,1)S(1)}, u32[]{:S(2)}, u32[]{:S(2)}) collective-permute-start(bf16[256,256]{1,0:T(8,128)(2,1)S(1)} %add_convert_fusion.4), channel_id=1, source_target_pairs={{16,0},{24,8},{32,16},{40,24},{48,32},{56,40},{64,48},{72,56},{80,... | collective-permute-start | bytes 393224 | tf_op jit(solution)/shard_map/ppermute | solution.py:294
  103.7 2.4 %collective-permute-start.21 = (bf16[128,256]{1,0:T(8,128)(2,1)S(1)}, bf16[128,256]{1,0:T(8,128)(2,1)S(1)}, u32[]{:S(2)}, u32[]{:S(2)}) collective-permute-start(bf16[128,256]{1,0:T(8,128)(2,1)S(1)} %get-tuple-element.34), channel_id=1, source_target_pairs={{0,8},{8,0},{16,24},{24,16},{32,40},{40,32},{48,56},{56,48},{64,72... | collective-permute-start | bytes 196616 | tf_op jit(solution)/shard_map/ppermute | solution.py:298
where the time goes:
time: 109 us; the launch traced here: 108 us
  waiting for transfers between devices  50.4 us (46%)
  starting transfers between devices  42.6 us (39%)
  Pallas kernels  12.3 us (11%)
    ppermute x16, waiting for transfers between devices, exchange(): return lax.ppermute(array, ('stretch', 'head'), pairs)  41.6 us
    ppermute x16, starting transfers between devices, exchange(): return lax.ppermute(array, ('stretch', 'head'), pairs)  25.4 us
    pallas_call x1, Pallas kernels, attend(): pl.pallas_call(attend_kernel, in_specs=[pl.BlockSpec(memory_space=pltpu.S...  10.7 us
    ppermute x1, starting transfers between devices, body(): swapped = lax.ppermute(swapped, 'stretch', swap)  6.74 us
    ppermute x1, waiting for transfers between devices, body(): sent_back = lax.ppermute(past_sum.astype(jnp.bfloat16), 'stretch', earlier)  5.95 us
    ppermute x1, starting transfers between devices, body(): past = lax.ppermute(own, 'stretch', later)  4.81 us
  transfers between devices with their start and end apart: 22, of which 15 were waited for; matrix products, arithmetic and copies ran while one was open for 1% of the time, Pallas kernels for 0%

commit v1 on v0

--- a/solution.py
+++ b/solution.py
@@ -204,7 +204,7 @@
     )(info, lengths, *operands)
 
 
-def join_kernel(info, att, dq, come, here, sent, other, att_out, dq_out, key_out, value_out):
+def place_kernel(info, att, dq, come, att_out, dq_out):
     core = lax.rem(info[1], 2)
     own = pl.multiple_of(core * WIDE, WIDE)
     far = pl.multiple_of((1 - core) * WIDE, WIDE)
@@ -212,6 +212,10 @@
     att_out[:, pl.ds(far, WIDE)] = come[:, :WIDE]
     dq_out[:, pl.ds(own, WIDE)] = dq[...]
     dq_out[:, pl.ds(far, WIDE)] = come[:, WIDE:]
+
+
+def join_kernel(info, here, sent, other, key_out, value_out):
+    core = lax.rem(info[1], 2)
     mine = (here[...] + sent[...].astype(jnp.float32)).astype(jnp.bfloat16)
     own = pl.multiple_of(core * HD, HD)
     far = pl.multiple_of((1 - core) * HD, HD)
@@ -221,17 +225,15 @@
     value_out[:, pl.ds(far, HD)] = other[:, HD:]
 
 
-def join(info, operands):
+def call(kernel, name, width, info, operands):
     whole = pl.BlockSpec(memory_space=pltpu.VMEM)
-    long = jax.ShapeDtypeStruct((ROWS, 2 * WIDE), jnp.bfloat16)
-    short = jax.ShapeDtypeStruct((ROWS, 2 * HD), jnp.bfloat16)
     return pl.pallas_call(
-        join_kernel,
+        kernel,
         in_specs=[pl.BlockSpec(memory_space=pltpu.SMEM)] + [whole] * len(operands),
-        out_specs=[whole] * 4,
-        out_shape=[long, long, short, short],
+        out_specs=[whole] * 2,
+        out_shape=[jax.ShapeDtypeStruct((ROWS, width), jnp.bfloat16)] * 2,
         compiler_params=pltpu.CompilerParams(vmem_limit_bytes=16 * 1024 * 1024),
-        name="join",
+        name=name,
     )(info, *operands)
 
 
@@ -295,8 +297,11 @@
     near, swapped = lax.optimization_barrier((near, outs[2]))
     here = here + exchange(near, above).astype(jnp.float32)
     swapped = lax.ppermute(swapped, "stretch", swap)
+    long = call(place_kernel, "place", 2 * WIDE, info, [outs[0], outs[1], swapped])
+    attended, query_grad, here = lax.optimization_barrier((*long, here))
     other = lax.ppermute(add(here[ROWS:], sent_back[ROWS:]), "stretch", swap)
-    return join(info, [outs[0], outs[1], swapped, here[:ROWS], sent_back[:ROWS], other])
+    short = call(join_kernel, "join", 2 * HD, info, [here[:ROWS], sent_back[:ROWS], other])
+    return attended, query_grad, *short
 
 
 def solution(mesh):

time: 109 us -> 109 us (level)
  starting transfers between devices: 42.6 us -> 50.9 us
  waiting for transfers between devices: 50.4 us -> 44.2 us
  Pallas kernels: 12.3 us -> 11 us
    ppermute x1, starting transfers between devices: 1.92 us -> 10.3 us  [body(): sent_back = lax.ppermute(past_sum.astype(jnp.bfloat16), 'stretch', earlier)]
    ppermute x1, waiting for transfers between devices: 5.95 us -> 0.27 us  [body(): sent_back = lax.ppermute(past_sum.astype(jnp.bfloat16), 'stretch', earlier)]
    ppermute x1, starting transfers between devices: 6.74 us -> 9.56 us  [body(): swapped = lax.ppermute(swapped, 'stretch', swap)]
    pallas_call x1, Pallas kernels: 10.7 us -> 8.19 us  [attend(): pl.pallas_call(attend_kernel, in_specs=[pl.BlockSpec(memory_space=pltpu.S...]
    ppermute x16, starting transfers between devices: 25.4 us -> 23.8 us  [exchange(): return lax.ppermute(array, ('stretch', 'head'), pairs)]
    ppermute x1, starting transfers between devices: 1.46 us -> 0.09 us  [body(): other = lax.ppermute(add(here[ROWS:], sent_back[ROWS:]), 'stretch', swap)]
    pallas_call x1 -> x2, Pallas kernels: 1.64 us -> 2.8 us  [call(): pl.pallas_call(kernel, in_specs=[pl.BlockSpec(memory_space=pltpu.SMEM)] +...]
  transfers between devices with their start and end apart: 22 -> 22, of which waited for: 15 -> 15; matrix products, arithmetic and copies ran while one was open for 1% -> 1% of each run, Pallas kernels for 0% -> 1%
where the time goes in v1:
time: 109 us; the launch traced here: 108 us
  starting transfers between devices  50.9 us (47%)
  waiting for transfers between devices  44.2 us (41%)
  Pallas kernels  11 us (10%)
    ppermute x16, waiting for transfers between devices, exchange(): return lax.ppermute(array, ('stretch', 'head'), pairs)  40.7 us
    ppermute x16, starting transfers between devices, exchange(): return lax.ppermute(array, ('stretch', 'head'), pairs)  23.8 us
    ppermute x1, starting transfers between devices, body(): sent_back = lax.ppermute(past_sum.astype(jnp.bfloat16), 'stretch', earlier)  10.3 us
    ppermute x1, starting transfers between devices, body(): swapped = lax.ppermute(swapped, 'stretch', swap)  9.56 us
    pallas_call x1, Pallas kernels, attend(): pl.pallas_call(attend_kernel, in_specs=[pl.BlockSpec(memory_space=pltpu.S...  8.19 us
    ppermute x1, starting transfers between devices, body(): past = lax.ppermute(own, 'stretch', later)  4.81 us
    pallas_call x2, Pallas kernels, call(): pl.pallas_call(kernel, in_specs=[pl.BlockSpec(memory_space=pltpu.SMEM)] +...  2.8 us
  transfers between devices with their start and end apart: 22, of which 15 were waited for; matrix products, arithmetic and copies ran while one was open for 1% of the time, Pallas kernels for 1%

profile of v1, /device:TPU:7, one launch (start us, length us, event | category | flops | bytes accessed | tf_op | source)
XLA Modules:
  0.0 108.4 jit_solution(7115463529219980896)
XLA Ops:
  0.6 0.8 constant_dynamic-slice_fusion.2
  1.5 0.8 collective-permute-start.1
  2.3 0.9 collective-permute-done.1
  3.2 5.7 %collective-permute-start.2 = (bf16[256,256]{1,0:T(8,128)(2,1)S(1)}, bf16[256,256]{1,0:T(8,128)(2,1)S(1)}, u32[]{:S(2)}, u32[]{:S(2)}) collective-permute-start(bf16[256,256]{1,0:T(8,128)(2,1)S(1)} %pad_maximum_fusion.2), channel_id=1, source_target_pairs={{0,1},{1,0},{2,3},{3,2},{4,5},{5,4},{6,7},{7,6},{8,15},{9,10},{10,... | collective-permute-start | bytes 393224 | tf_op jit(solution)/shard_map/ppermute | solution.py:264
  8.8 4.8 %collective-permute-start.6 = (bf16[256,256]{1,0:T(8,128)(2,1)S(1)}, bf16[256,256]{1,0:T(8,128)(2,1)S(1)}, u32[]{:S(2)}, u32[]{:S(2)}) collective-permute-start(bf16[256,256]{1,0:T(8,128)(2,1)S(1)} %pad_maximum_fusion.2), channel_id=1, source_target_pairs={{0,16},{8,24},{16,32},{24,40},{32,48},{40,56},{48,64},{56,72},{64,... | collective-permute-start | bytes 393224 | tf_op jit(solution)/shard_map/ppermute | solution.py:287
  13.7 0.0 copy-start.2
  13.7 0.0 copy-start
  13.7 2.1 %collective-permute-start.7 = (bf16[256,256]{1,0:T(8,128)(2,1)S(1)}, bf16[256,256]{1,0:T(8,128)(2,1)S(1)}, u32[]{:S(2)}, u32[]{:S(2)}) collective-permute-start(bf16[256,256]{1,0:T(8,128)(2,1)S(1)} %pad_maximum_fusion.2), channel_id=1, source_target_pairs={{0,17},{1,16},{2,19},{3,18},{4,21},{5,20},{6,23},{7,22},{8,31},{9,... | collective-permute-start | bytes 393224 | tf_op jit(solution)/shard_map/ppermute | solution.py:264
  15.7 0.0 collective-permute-done.2
  15.8 0.1 collective-permute-start.3
  15.9 1.1 collective-permute-done.6
  17.0 8.2 %collective-permute-done.7 = bf16[256,256]{1,0:T(8,128)(2,1)S(1)} collective-permute-done((bf16[256,256]{1,0:T(8,128)(2,1)S(1)}, bf16[256,256]{1,0:T(8,128)(2,1)S(1)}, u32[]{:S(2)}, u32[]{:S(2)}) %collective-permute-start.7) | collective-permute-done | bytes 131104 | tf_op jit(solution)/shard_map/ppermute | solution.py:264
  25.1 0.1 collective-permute-start.8
  25.2 0.0 copy-done.2
  25.2 0.0 copy-done
  25.3 1.5 %collective-permute-start = (bf16[128,2048]{1,0:T(8,128)(2,1)S(1)}, bf16[128,2048]{1,0:T(8,128)(2,1)}, u32[]{:S(2)}, u32[]{:S(2)}) collective-permute-start(bf16[128,2048]{1,0:T(8,128)(2,1)S(1)} %pad_maximum_fusion), channel_id=1, source_target_pairs={{0,8},{8,0},{16,24},{24,16},{32,40},{40,32},{48,56},{56,48},{64,72... | collective-permute-start | bytes 1572872 | tf_op jit(solution)/shard_map/ppermute | solution.py:286
  26.9 0.0 collective-permute-done.3.refs_1_
  26.9 0.0 collective-permute-start.4
  26.9 4.3 %collective-permute-done.8.refs_5_ = bf16[512,256]{1,0:T(8,128)(2,1)S(1)} collective-permute-done((bf16[512,256]{1,0:T(8,128)(2,1)S(1)}, bf16[512,256]{1,0:T(8,128)(2,1)S(1)}, u32[]{:S(2)}, u32[]{:S(2)}) %collective-permute-start.8) | collective-permute-done | bytes 262176 | tf_op jit(solution)/shard_map/ppermute | solution.py:264
  31.2 0.0 collective-permute-start.9
  31.2 2.1 %collective-permute-done.4.refs_2_ = bf16[512,256]{1,0:T(8,128)(2,1)S(1)} collective-permute-done((bf16[512,256]{1,0:T(8,128)(2,1)S(1)}, bf16[512,256]{1,0:T(8,128)(2,1)S(1)}, u32[]{:S(2)}, u32[]{:S(2)}) %collective-permute-start.4) | collective-permute-done | bytes 262176 | tf_op jit(solution)/shard_map/ppermute | solution.py:264
  33.3 0.0 collective-permute-start.5
  33.3 4.3 %collective-permute-done.9.refs_6_ = bf16[512,256]{1,0:T(8,128)(2,1)S(1)} collective-permute-done((bf16[512,256]{1,0:T(8,128)(2,1)S(1)}, bf16[512,256]{1,0:T(8,128)(2,1)S(1)}, u32[]{:S(2)}, u32[]{:S(2)}) %collective-permute-start.9) | collective-permute-done | bytes 262176 | tf_op jit(solution)/shard_map/ppermute | solution.py:264
  37.7 0.0 collective-permute-start.10
  37.7 0.0 copy-start.1
  37.7 0.1 pad_add_fusion.info
  37.7 0.0 collective-permute-done.come
  37.7 3.4 %collective-permute-done.5.refs_3_ = bf16[512,256]{1,0:T(8,128)(2,1)S(1)} collective-permute-done((bf16[512,256]{1,0:T(8,128)(2,1)S(1)}, bf16[512,256]{1,0:T(8,128)(2,1)S(1)}, u32[]{:S(2)}, u32[]{:S(2)}) %collective-permute-start.5) | collective-permute-done | bytes 262176 | tf_op jit(solution)/shard_map/ppermute | solution.py:264
  41.2 3.0 %collective-permute-done.10.refs_7_ = bf16[512,256]{1,0:T(8,128)(2,1)S(1)} collective-permute-done((bf16[512,256]{1,0:T(8,128)(2,1)S(1)}, bf16[512,256]{1,0:T(8,128)(2,1)S(1)}, u32[]{:S(2)}, u32[]{:S(2)}) %collective-permute-start.10) | collective-permute-done | bytes 262176 | tf_op jit(solution)/shard_map/ppermute | solution.py:264
  44.2 0.0 copy-done.1
  44.2 8.2 %attend.1 = (bf16[128,1024]{1,0:T(8,128)(2,1)S(1)}, bf16[128,1024]{1,0:T(8,128)(2,1)S(1)}, bf16[128,2048]{1,0:T(8,128)(2,1)S(1)}, f32[256,256]{1,0:T(8,128)S(1)}...) custom-call(s32[2]{0:T(128)S(1)} %pad_add_fusion.info, ...), custom_call_target="tpu_custom_call" | custom-call | tf_op jit(solution)/shard_map/attend/pallas_call | solution.py:181
  52.4 0.1 collective-permute-start.16
  52.5 1.5 %collective-permute-start.11 = (bf16[512,256]{1,0:T(8,128)(2,1)S(1)}, bf16[512,256]{1,0:T(8,128)(2,1)S(1)}, u32[]{:S(2)}, u32[]{:S(2)}) collective-permute-start(bf16[512,256]{1,0:T(8,128)(2,1)S(1)} %get-tuple-element.31), channel_id=1, source_target_pairs={{0,7},{1,2},{2,1},{3,4},{4,3},{5,6},{6,5},{7,0},{8,9},{9,8},{10,11... | collective-permute-start | bytes 786440 | tf_op jit(solution)/shard_map/ppermute | solution.py:264
  53.9 3.8 %collective-permute-done.16 = bf16[512,256]{1,0:T(8,128)(2,1)S(1)} collective-permute-done((bf16[512,256]{1,0:T(8,128)(2,1)S(1)}, bf16[512,256]{1,0:T(8,128)(2,1)S(1)}, u32[]{:S(2)}, u32[]{:S(2)}) %collective-permute-start.16) | collective-permute-done | bytes 262176 | tf_op jit(solution)/shard_map/ppermute | solution.py:264
  57.7 0.1 add_convert_fusion.1
  57.7 3.7 %collective-permute-start.17 = (bf16[512,256]{1,0:T(8,128)(2,1)S(1)}, bf16[512,256]{1,0:T(8,128)(2,1)S(1)}, u32[]{:S(2)}, u32[]{:S(2)}) collective-permute-start(bf16[512,256]{1,0:T(8,128)(2,1)S(1)} %add_convert_fusion.1), channel_id=1, source_target_pairs={{0,1},{1,0},{2,3},{3,2},{4,5},{5,4},{6,7},{7,6},{8,15},{9,10},{10,... | collective-permute-start | bytes 786440 | tf_op jit(solution)/shard_map/ppermute | solution.py:264
  61.5 0.0 collective-permute-done.11
  61.5 0.1 add_convert_fusion.3
  61.5 2.7 %collective-permute-start.12 = (bf16[512,256]{1,0:T(8,128)(2,1)S(1)}, bf16[512,256]{1,0:T(8,128)(2,1)S(1)}, u32[]{:S(2)}, u32[]{:S(2)}) collective-permute-start(bf16[512,256]{1,0:T(8,128)(2,1)S(1)} %add_convert_fusion.3), channel_id=1, source_target_pairs={{0,1},{1,0},{2,3},{3,2},{4,5},{5,4},{6,7},{7,6},{8,15},{9,10},{10,... | collective-permute-start | bytes 786440 | tf_op jit(solution)/shard_map/ppermute | solution.py:264
  64.3 3.6 %collective-permute-done.17 = bf16[512,256]{1,0:T(8,128)(2,1)S(1)} collective-permute-done((bf16[512,256]{1,0:T(8,128)(2,1)S(1)}, bf16[512,256]{1,0:T(8,128)(2,1)S(1)}, u32[]{:S(2)}, u32[]{:S(2)}) %collective-permute-start.17) | collective-permute-done | bytes 262176 | tf_op jit(solution)/shard_map/ppermute | solution.py:264
  67.9 0.1 add_convert_fusion
  67.9 0.3 collective-permute-start.18
  68.3 5.2 %collective-permute-done.12 = bf16[512,256]{1,0:T(8,128)(2,1)S(1)} collective-permute-done((bf16[512,256]{1,0:T(8,128)(2,1)S(1)}, bf16[512,256]{1,0:T(8,128)(2,1)S(1)}, u32[]{:S(2)}, u32[]{:S(2)}) %collective-permute-start.12) | collective-permute-done | bytes 262176 | tf_op jit(solution)/shard_map/ppermute | solution.py:264
  73.5 0.1 add_convert_fusion.2
  73.6 0.1 collective-permute-start.13
  73.7 1.3 %collective-permute-done.18 = bf16[512,256]{1,0:T(8,128)(2,1)S(1)} collective-permute-done((bf16[512,256]{1,0:T(8,128)(2,1)S(1)}, bf16[512,256]{1,0:T(8,128)(2,1)S(1)}, u32[]{:S(2)}, u32[]{:S(2)}) %collective-permute-start.18) | collective-permute-done | bytes 262176 | tf_op jit(solution)/shard_map/ppermute | solution.py:264
  75.0 4.6 %collective-permute-start.19 = (bf16[256,256]{1,0:T(8,128)(2,1)S(1)}, bf16[256,256]{1,0:T(8,128)(2,1)S(1)}, u32[]{:S(2)}, u32[]{:S(2)}) collective-permute-start(bf16[256,256]{1,0:T(8,128)(2,1)S(1)} %add_convert_fusion.5), channel_id=1, source_target_pairs={{0,1},{1,0},{2,3},{3,2},{4,5},{5,4},{6,7},{7,6},{8,15},{9,10},{10,... | collective-permute-start | bytes 393224 | tf_op jit(solution)/shard_map/ppermute | solution.py:264
  79.5 1.5 %collective-permute-done.13 = bf16[512,256]{1,0:T(8,128)(2,1)S(1)} collective-permute-done((bf16[512,256]{1,0:T(8,128)(2,1)S(1)}, bf16[512,256]{1,0:T(8,128)(2,1)S(1)}, u32[]{:S(2)}, u32[]{:S(2)}) %collective-permute-start.13) | collective-permute-done | bytes 262176 | tf_op jit(solution)/shard_map/ppermute | solution.py:264
  81.1 9.6 %collective-permute-start.14 = (bf16[128,2048]{1,0:T(8,128)(2,1)S(1)}, bf16[128,2048]{1,0:T(8,128)(2,1)S(1)}, u32[]{:S(2)}, u32[]{:S(2)}) collective-permute-start(bf16[128,2048]{1,0:T(8,128)(2,1)S(1)} %get-tuple-element.33), channel_id=1, source_target_pairs={{0,8},{8,0},{16,24},{24,16},{32,40},{40,32},{48,56},{56,48},{64,72... | collective-permute-start | bytes 1572872 | tf_op jit(solution)/shard_map/ppermute | solution.py:299
  90.6 3.0 %collective-permute-start.15 = (bf16[256,256]{1,0:T(8,128)(2,1)S(1)}, bf16[256,256]{1,0:T(8,128)(2,1)S(1)}, u32[]{:S(2)}, u32[]{:S(2)}) collective-permute-start(bf16[256,256]{1,0:T(8,128)(2,1)S(1)} %add_convert_fusion.6), channel_id=1, source_target_pairs={{0,1},{1,0},{2,3},{3,2},{4,5},{5,4},{6,7},{7,6},{8,15},{9,10},{10,... | collective-permute-start | bytes 393224 | tf_op jit(solution)/shard_map/ppermute | solution.py:264
  93.6 0.0 collective-permute-done.19
  93.6 10.3 %collective-permute-start.20 = (bf16[256,256]{1,0:T(8,128)(2,1)S(1)}, bf16[256,256]{1,0:T(8,128)(2,1)S(1)}, u32[]{:S(2)}, u32[]{:S(2)}) collective-permute-start(bf16[256,256]{1,0:T(8,128)(2,1)S(1)} %add_convert_fusion.4), channel_id=1, source_target_pairs={{16,0},{24,8},{32,16},{40,24},{48,32},{56,40},{64,48},{72,56},{80,... | collective-permute-start | bytes 393224 | tf_op jit(solution)/shard_map/ppermute | solution.py:296
  103.9 0.0 collective-permute-done.15
  104.0 0.0 collective-permute-done.14.come
  104.0 1.6 %place.1 = (bf16[128,2048]{1,0:T(8,128)(2,1)}, bf16[128,2048]{1,0:T(8,128)(2,1)}) custom-call(s32[2]{0:T(128)S(1)} %pad_add_fusion.info, bf16[128,1024]{1,0:T(8,128)(2,1)S(1)} %get-tuple-element.26.att, bf16[128,1024]{1,0:T(8,128)(2,1)S(1)} %get-tuple-element.27.dq, bf16[128,2048]{1,0:T(8,128)(2,1)S(1)} %collective-permute-done.14.come), custom_call_target="tpu_custom_call" | custom-call | tf_op jit(solution)/shard_map/place/pallas_call | solution.py:230
  105.6 0.3 collective-permute-done.20
  105.9 0.1 collective-permute-start.21
  106.0 1.2 %collective-permute-done.21.other = bf16[128,256]{1,0:T(8,128)(2,1)S(1)} collective-permute-done((bf16[128,256]{1,0:T(8,128)(2,1)S(1)}, bf16[128,256]{1,0:T(8,128)(2,1)S(1)}, u32[]{:S(2)}, u32[]{:S(2)}) %collective-permute-start.21) | collective-permute-done | bytes 65568 | tf_op jit(solution)/shard_map/ppermute | solution.py:302
  107.2 1.2 %join.1 = (bf16[128,256]{1,0:T(8,128)(2,1)}, bf16[128,256]{1,0:T(8,128)(2,1)}) custom-call(s32[2]{0:T(128)S(1)} %pad_add_fusion.info, f32[128,256]{1,0:T(8,128)S(1)} %get-tuple-element.49.here, bf16[128,256]{1,0:T(8,128)(2,1)S(1)} %slice.36.sent, bf16[128,256]{1,0:T(8,128)(2,1)S(1)} %collective-permute-done.21.other), custom_call_target="tpu_custom_call" | custom-call | tf_op jit(solution)/shard_map/join/pallas_call | solution.py:230
  (13 shorter events, 0.3 us)
Async XLA Ops:
  1.5 1.7 %collective-permute-start.1 = (bf16[128,256]{1,0:T(8,128)(2,1)S(1)}, bf16[128,256]{1,0:T(8,128)(2,1)S(1)}, u32[]{:S(2)}, u32[]{:S(2)}) collective-permute-start(bf16[128,256]{1,0:T(8,128)(2,1)S(1)} %pad_maximum_fusion.3), channel_id=1, source_target_pairs={{0,8},{8,0},{16,24},{24,16},{32,40},{40,32},{48,56},{56,48},{64,72... | collective-permute-start | bytes 196616 | tf_op jit(solution)/shard_map/ppermute | solution.py:284
  3.2 12.6 %collective-permute-start.2 = (bf16[256,256]{1,0:T(8,128)(2,1)S(1)}, bf16[256,256]{1,0:T(8,128)(2,1)S(1)}, u32[]{:S(2)}, u32[]{:S(2)}) collective-permute-start(bf16[256,256]{1,0:T(8,128)(2,1)S(1)} %pad_maximum_fusion.2), channel_id=1, source_target_pairs={{0,1},{1,0},{2,3},{3,2},{4,5},{5,4},{6,7},{7,6},{8,15},{9,10},{10,... | collective-permute-start | bytes 393224 | tf_op jit(solution)/shard_map/ppermute | solution.py:264
  8.8 8.1 %collective-permute-start.6 = (bf16[256,256]{1,0:T(8,128)(2,1)S(1)}, bf16[256,256]{1,0:T(8,128)(2,1)S(1)}, u32[]{:S(2)}, u32[]{:S(2)}) collective-permute-start(bf16[256,256]{1,0:T(8,128)(2,1)S(1)} %pad_maximum_fusion.2), channel_id=1, source_target_pairs={{0,16},{8,24},{16,32},{24,40},{32,48},{40,56},{48,64},{56,72},{64,... | collective-permute-start | bytes 393224 | tf_op jit(solution)/shard_map/ppermute | solution.py:287
  13.7 11.6 %copy-start.2 = (bf16[128,2048]{1,0:T(8,128)(2,1)S(1)}, bf16[128,2048]{1,0:T(8,128)(2,1)}, u32[]{:S(2)}) copy-start(bf16[128,2048]{1,0:T(8,128)(2,1)} %go.1) | copy-start | bytes 1572868
  13.7 11.6 %copy-start = (bf16[128,2048]{1,0:T(8,128)(2,1)S(1)}, bf16[128,2048]{1,0:T(8,128)(2,1)}, u32[]{:S(2)}) copy-start(bf16[128,2048]{1,0:T(8,128)(2,1)} %qo.1) | copy-start | bytes 1572868
  13.7 11.4 %collective-permute-start.7 = (bf16[256,256]{1,0:T(8,128)(2,1)S(1)}, bf16[256,256]{1,0:T(8,128)(2,1)S(1)}, u32[]{:S(2)}, u32[]{:S(2)}) collective-permute-start(bf16[256,256]{1,0:T(8,128)(2,1)S(1)} %pad_maximum_fusion.2), channel_id=1, source_target_pairs={{0,17},{1,16},{2,19},{3,18},{4,21},{5,20},{6,23},{7,22},{8,31},{9,... | collective-permute-start | bytes 393224 | tf_op jit(solution)/shard_map/ppermute | solution.py:264
  15.8 11.1 %collective-permute-start.3 = (bf16[512,256]{1,0:T(8,128)(2,1)S(1)}, bf16[512,256]{1,0:T(8,128)(2,1)S(1)}, u32[]{:S(2)}, u32[]{:S(2)}) collective-permute-start(bf16[512,256]{1,0:T(8,128)(2,1)S(1)} %pad_maximum_fusion.1.refs_0_), channel_id=1, source_target_pairs={{0,7},{1,2},{2,1},{3,4},{4,3},{5,6},{6,5},{7,0},{8,9},{9,8},{10,11... | collective-permute-start | bytes 786440 | tf_op jit(solution)/shard_map/ppermute | solution.py:264
  25.1 6.1 %collective-permute-start.8 = (bf16[512,256]{1,0:T(8,128)(2,1)S(1)}, bf16[512,256]{1,0:T(8,128)(2,1)S(1)}, u32[]{:S(2)}, u32[]{:S(2)}) collective-permute-start(bf16[512,256]{1,0:T(8,128)(2,1)S(1)} %constant_dynamic-update-slice_fusion.refs_4_), channel_id=1, source_target_pairs={{0,7},{1,2},{2,1},{3,4},{4,3},{5,6},{6,5},{7,0},{8,9},{9,8},{10,11... | collective-permute-start | bytes 786440 | tf_op jit(solution)/shard_map/ppermute | solution.py:264
  25.3 12.4 %collective-permute-start = (bf16[128,2048]{1,0:T(8,128)(2,1)S(1)}, bf16[128,2048]{1,0:T(8,128)(2,1)}, u32[]{:S(2)}, u32[]{:S(2)}) collective-permute-start(bf16[128,2048]{1,0:T(8,128)(2,1)S(1)} %pad_maximum_fusion), channel_id=1, source_target_pairs={{0,8},{8,0},{16,24},{24,16},{32,40},{40,32},{48,56},{56,48},{64,72... | collective-permute-start | bytes 1572872 | tf_op jit(solution)/shard_map/ppermute | solution.py:286
  26.9 6.4 %collective-permute-start.4 = (bf16[512,256]{1,0:T(8,128)(2,1)S(1)}, bf16[512,256]{1,0:T(8,128)(2,1)S(1)}, u32[]{:S(2)}, u32[]{:S(2)}) collective-permute-start(bf16[512,256]{1,0:T(8,128)(2,1)S(1)} %collective-permute-done.3.refs_1_), channel_id=1, source_target_pairs={{0,1},{1,0},{2,3},{3,2},{4,5},{5,4},{6,7},{7,6},{8,15},{9,10},{10,... | collective-permute-start | bytes 786440 | tf_op jit(solution)/shard_map/ppermute | solution.py:264
  31.2 6.4 %collective-permute-start.9 = (bf16[512,256]{1,0:T(8,128)(2,1)S(1)}, bf16[512,256]{1,0:T(8,128)(2,1)S(1)}, u32[]{:S(2)}, u32[]{:S(2)}) collective-permute-start(bf16[512,256]{1,0:T(8,128)(2,1)S(1)} %collective-permute-done.8.refs_5_), channel_id=1, source_target_pairs={{0,1},{1,0},{2,3},{3,2},{4,5},{5,4},{6,7},{7,6},{8,15},{9,10},{10,... | collective-permute-start | bytes 786440 | tf_op jit(solution)/shard_map/ppermute | solution.py:264
  33.3 7.9 %collective-permute-start.5 = (bf16[512,256]{1,0:T(8,128)(2,1)S(1)}, bf16[512,256]{1,0:T(8,128)(2,1)S(1)}, u32[]{:S(2)}, u32[]{:S(2)}) collective-permute-start(bf16[512,256]{1,0:T(8,128)(2,1)S(1)} %collective-permute-done.4.refs_2_), channel_id=1, source_target_pairs={{0,7},{1,2},{2,1},{3,4},{4,3},{5,6},{6,5},{7,0},{8,9},{9,8},{10,11... | collective-permute-start | bytes 786440 | tf_op jit(solution)/shard_map/ppermute | solution.py:264
  37.7 6.5 %collective-permute-start.10 = (bf16[512,256]{1,0:T(8,128)(2,1)S(1)}, bf16[512,256]{1,0:T(8,128)(2,1)S(1)}, u32[]{:S(2)}, u32[]{:S(2)}) collective-permute-start(bf16[512,256]{1,0:T(8,128)(2,1)S(1)} %collective-permute-done.9.refs_6_), channel_id=1, source_target_pairs={{0,7},{1,2},{2,1},{3,4},{4,3},{5,6},{6,5},{7,0},{8,9},{9,8},{10,11... | collective-permute-start | bytes 786440 | tf_op jit(solution)/shard_map/ppermute | solution.py:264
  37.7 6.5 %copy-start.1 = (s32[64]{0:T(128)S(1)}, s32[64]{0:T(128)}, u32[]{:S(2)}) copy-start(s32[64]{0:T(128)} %lengths.1) | copy-start | bytes 772
  52.4 5.3 %collective-permute-start.16 = (bf16[512,256]{1,0:T(8,128)(2,1)S(1)}, bf16[512,256]{1,0:T(8,128)(2,1)S(1)}, u32[]{:S(2)}, u32[]{:S(2)}) collective-permute-start(bf16[512,256]{1,0:T(8,128)(2,1)S(1)} %get-tuple-element.44), channel_id=1, source_target_pairs={{0,7},{1,2},{2,1},{3,4},{4,3},{5,6},{6,5},{7,0},{8,9},{9,8},{10,11... | collective-permute-start | bytes 786440 | tf_op jit(solution)/shard_map/ppermute | solution.py:264
  52.5 9.0 %collective-permute-start.11 = (bf16[512,256]{1,0:T(8,128)(2,1)S(1)}, bf16[512,256]{1,0:T(8,128)(2,1)S(1)}, u32[]{:S(2)}, u32[]{:S(2)}) collective-permute-start(bf16[512,256]{1,0:T(8,128)(2,1)S(1)} %get-tuple-element.31), channel_id=1, source_target_pairs={{0,7},{1,2},{2,1},{3,4},{4,3},{5,6},{6,5},{7,0},{8,9},{9,8},{10,11... | collective-permute-start | bytes 786440 | tf_op jit(solution)/shard_map/ppermute | solution.py:264
  57.7 10.1 %collective-permute-start.17 = (bf16[512,256]{1,0:T(8,128)(2,1)S(1)}, bf16[512,256]{1,0:T(8,128)(2,1)S(1)}, u32[]{:S(2)}, u32[]{:S(2)}) collective-permute-start(bf16[512,256]{1,0:T(8,128)(2,1)S(1)} %add_convert_fusion.1), channel_id=1, source_target_pairs={{0,1},{1,0},{2,3},{3,2},{4,5},{5,4},{6,7},{7,6},{8,15},{9,10},{10,... | collective-permute-start | bytes 786440 | tf_op jit(solution)/shard_map/ppermute | solution.py:264
  61.5 11.9 %collective-permute-start.12 = (bf16[512,256]{1,0:T(8,128)(2,1)S(1)}, bf16[512,256]{1,0:T(8,128)(2,1)S(1)}, u32[]{:S(2)}, u32[]{:S(2)}) collective-permute-start(bf16[512,256]{1,0:T(8,128)(2,1)S(1)} %add_convert_fusion.3), channel_id=1, source_target_pairs={{0,1},{1,0},{2,3},{3,2},{4,5},{5,4},{6,7},{7,6},{8,15},{9,10},{10,... | collective-permute-start | bytes 786440 | tf_op jit(solution)/shard_map/ppermute | solution.py:264
  67.9 7.0 %collective-permute-start.18 = (bf16[512,256]{1,0:T(8,128)(2,1)S(1)}, bf16[512,256]{1,0:T(8,128)(2,1)S(1)}, u32[]{:S(2)}, u32[]{:S(2)}) collective-permute-start(bf16[512,256]{1,0:T(8,128)(2,1)S(1)} %add_convert_fusion), channel_id=1, source_target_pairs={{0,7},{1,2},{2,1},{3,4},{4,3},{5,6},{6,5},{7,0},{8,9},{9,8},{10,11... | collective-permute-start | bytes 786440 | tf_op jit(solution)/shard_map/ppermute | solution.py:264
  73.6 7.5 %collective-permute-start.13 = (bf16[512,256]{1,0:T(8,128)(2,1)S(1)}, bf16[512,256]{1,0:T(8,128)(2,1)S(1)}, u32[]{:S(2)}, u32[]{:S(2)}) collective-permute-start(bf16[512,256]{1,0:T(8,128)(2,1)S(1)} %add_convert_fusion.2), channel_id=1, source_target_pairs={{0,7},{1,2},{2,1},{3,4},{4,3},{5,6},{6,5},{7,0},{8,9},{9,8},{10,11... | collective-permute-start | bytes 786440 | tf_op jit(solution)/shard_map/ppermute | solution.py:264
  75.0 18.6 %collective-permute-start.19 = (bf16[256,256]{1,0:T(8,128)(2,1)S(1)}, bf16[256,256]{1,0:T(8,128)(2,1)S(1)}, u32[]{:S(2)}, u32[]{:S(2)}) collective-permute-start(bf16[256,256]{1,0:T(8,128)(2,1)S(1)} %add_convert_fusion.5), channel_id=1, source_target_pairs={{0,1},{1,0},{2,3},{3,2},{4,5},{5,4},{6,7},{7,6},{8,15},{9,10},{10,... | collective-permute-start | bytes 393224 | tf_op jit(solution)/shard_map/ppermute | solution.py:264
  81.1 22.9 %collective-permute-start.14 = (bf16[128,2048]{1,0:T(8,128)(2,1)S(1)}, bf16[128,2048]{1,0:T(8,128)(2,1)S(1)}, u32[]{:S(2)}, u32[]{:S(2)}) collective-permute-start(bf16[128,2048]{1,0:T(8,128)(2,1)S(1)} %get-tuple-element.33), channel_id=1, source_target_pairs={{0,8},{8,0},{16,24},{24,16},{32,40},{40,32},{48,56},{56,48},{64,72... | collective-permute-start | bytes 1572872 | tf_op jit(solution)/shard_map/ppermute | solution.py:299
  90.6 13.3 %collective-permute-start.15 = (bf16[256,256]{1,0:T(8,128)(2,1)S(1)}, bf16[256,256]{1,0:T(8,128)(2,1)S(1)}, u32[]{:S(2)}, u32[]{:S(2)}) collective-permute-start(bf16[256,256]{1,0:T(8,128)(2,1)S(1)} %add_convert_fusion.6), channel_id=1, source_target_pairs={{0,1},{1,0},{2,3},{3,2},{4,5},{5,4},{6,7},{7,6},{8,15},{9,10},{10,... | collective-permute-start | bytes 393224 | tf_op jit(solution)/shard_map/ppermute | solution.py:264
  93.6 12.2 %collective-permute-start.20 = (bf16[256,256]{1,0:T(8,128)(2,1)S(1)}, bf16[256,256]{1,0:T(8,128)(2,1)S(1)}, u32[]{:S(2)}, u32[]{:S(2)}) collective-permute-start(bf16[256,256]{1,0:T(8,128)(2,1)S(1)} %add_convert_fusion.4), channel_id=1, source_target_pairs={{16,0},{24,8},{32,16},{40,24},{48,32},{56,40},{64,48},{72,56},{80,... | collective-permute-start | bytes 393224 | tf_op jit(solution)/shard_map/ppermute | solution.py:296
  105.9 1.3 %collective-permute-start.21 = (bf16[128,256]{1,0:T(8,128)(2,1)S(1)}, bf16[128,256]{1,0:T(8,128)(2,1)S(1)}, u32[]{:S(2)}, u32[]{:S(2)}) collective-permute-start(bf16[128,256]{1,0:T(8,128)(2,1)S(1)} %get-tuple-element.48), channel_id=1, source_target_pairs={{0,8},{8,0},{16,24},{24,16},{32,40},{40,32},{48,56},{56,48},{64,72... | collective-permute-start | bytes 196616 | tf_op jit(solution)/shard_map/ppermute | solution.py:302
